TPU v7x, 512 devices: a whole 4x8x8 slice. The times are simulated.
512 devices in a mesh: re: 16 (over y, core), pb: 32 (over x, z).
Axes of the slice: x: 4, y: 8, z: 8, core: 2. Of those that a mesh axis runs over, the one named last changes fastest.
Arguments:
- wannier_coupling: float32 [512, 4, 32, 3072], P('re', None, 'pb'), may hold values from -0.125 to 0.125
- electron_cells: int32 [3, 512], P(None, 're'), may hold values from -6 to 6
- phonon_cells: int32 [3, 4], replicated, may hold values from -6 to 6
- kpoint_coords: int32 [3, 8], replicated, may hold values from 0 to 7
- qpoint_coords: int32 [3, 128], replicated, may hold values from 0 to 7
- band_rotations: float32 [512, 2048], P('pb'), may hold values from -0.75 to 0.75
- mode_vectors: float32 [128, 4608], P('pb'), may hold values from -0.625 to 0.625
Outputs:
- coupling: float32 [8, 128, 32, 3072], P(None, 'pb', 're')
All inputs are finite; a program needn't handle non-finite values.
Results may differ from a plain program's by a relative error of at most 0.000098.
Values sent between devices are 32-bit elements; how exact they have to be, the bound alone decides.
A program may use at most 64 MiB of HBM per device.

v0:
```python
import math

import jax
import jax.numpy as jnp
from jax import lax
from jax.experimental import pallas as pl
from jax.experimental.pallas import tpu as pltpu
from jax.sharding import PartitionSpec as P

f32, bf16, i32 = jnp.float32, jnp.bfloat16, jnp.int32
MESH = pl.DeviceIdType.MESH
NN = ((1,), (0,))
NT = ((1,), (1,))


def split(value):
    high = value.astype(bf16)
    return high, (value - high.astype(f32)).astype(bf16)


def dot(left, right, dims):
    return lax.dot_general(left, right, (dims, ((), ())), preferred_element_type=f32)


def dot3(left, right, dims):
    return (
        dot(left[0], right[0], dims) + dot(left[1], right[0], dims) + dot(left[0], right[1], dims)
    )


def iota(shape, axis):
    return lax.broadcasted_iota(i32, shape, axis)


def wave(turns, period):
    cosine = jnp.zeros(turns.shape, f32)
    sine = jnp.zeros(turns.shape, f32)
    for step in range(period):
        hit = turns == step
        angle = 2 * math.pi * step / period
        cosine = jnp.where(hit, jnp.float32(math.cos(angle)), cosine)
        sine = jnp.where(hit, jnp.float32(math.sin(angle)), sine)
    return cosine, sine


def unfold(slices, wide):
    group = iota((16, 128), 1) >> 5
    for j in range(4):
        wide[pl.ds(j, 16, stride=4), :] = jnp.where(group == j, slices, 0.0)
    kept = wide[...]
    kept = kept + pltpu.roll(kept, 64, 1)
    return kept + pltpu.roll(kept, 32, 1)


def kernel(
    g_hbm, cells, pcell, kco, qco, rot_hbm, modes, out,
    g, acc, ra1, ra2, table, sel, usk, usq, wide, gkpad, a3s, a3r, xs,
    fq, fh, fl, bh, bl, xh, xl, ys,
    gsem, tsem, u1zs, u1zr, u1xs, u1xr, a1s_sem, a1r_sem, a2s_sem, a2r_sem,
    uks, ukr, uqs, uqr, ufs, ufr, a3s_sem, a3r_sem, bzs, bzr, bxs, bxr,
):
    re = lax.axis_index("re")
    pb = lax.axis_index("pb")
    y, core = re // 2, re % 2
    x, z = pb // 8, pb % 8

    def remote(src, dst, ssem, rsem, to_re, to_pb):
        return pltpu.make_async_remote_copy(
            src_ref=src, dst_ref=dst, send_sem=ssem, recv_sem=rsem,
            device_id=(to_re, to_pb), device_id_type=MESH,
        )

    def each(count, body):
        def step(i, carry):
            body(i)
            return carry

        lax.fori_loop(0, count, step, 0)

    g_copy = pltpu.make_async_copy(g_hbm, g, gsem.at[0])
    g_copy.start()
    own_rows = table.at[pl.ds(pl.multiple_of(pb * 16, 16), 16), :]
    t_copy = pltpu.make_async_copy(
        rot_hbm.at[:, pl.ds(pl.multiple_of(re * 128, 128), 128)], own_rows, tsem.at[0]
    )
    t_copy.start()

    barrier = pltpu.get_barrier_semaphore()

    def greet_re(d):
        pl.semaphore_signal(barrier, 1, device_id=((re + d + 1) % 16, pb), device_id_type=MESH)

    def greet_z(d):
        pl.semaphore_signal(
            barrier, 1, device_id=(re, x * 8 + (z + d + 1) % 8), device_id_type=MESH
        )

    def greet_x(d):
        pl.semaphore_signal(
            barrier, 1, device_id=(re, ((x + d + 1) % 4) * 8 + z), device_id_type=MESH
        )

    each(15, greet_re)
    each(7, greet_z)
    each(3, greet_x)

    row = iota((8, 32), 0)
    turns = jnp.zeros((8, 32), i32)
    for d in range(3):
        coef = jnp.zeros((8, 32), i32)
        for k in range(8):
            coef = jnp.where(row == k, 2 * kco[d, k] + 1, coef)
        turns = turns + coef * jnp.broadcast_to(cells[d : d + 1, :], (8, 32))
    cosine, sine = wave(turns & 15, 16)
    waves_h, waves_l = split(jnp.concatenate([cosine, sine], axis=0))
    waves = jnp.concatenate([waves_h, waves_l], axis=0)

    pl.semaphore_wait(barrier, 25)
    t_copy.wait()

    def u1z(d):
        return remote(
            own_rows, own_rows, u1zs.at[d], u1zr.at[z], re, x * 8 + (z + d + 1) % 8
        )

    each(7, lambda d: u1z(d).start())
    g_copy.wait()

    odd = ((iota((8, 128), 1) >> 5) & 1) == 1

    def phase_half(half):
        def step(i):
            for pp in range(2):
                highs, lows = [], []
                for lo in range(2):
                    start = half * 48 + pp * 24 + 2 * i + lo
                    high, low = split(g[pl.ds(start, 32, stride=96), :])
                    highs.append(high)
                    lows.append(low)
                high = jnp.concatenate(highs, axis=1)
                low = jnp.concatenate(lows, axis=1)
                first = dot(waves, high, NN)
                both = first[0:16] + first[16:32] + dot(waves_h, low, NN)
                for lo in range(2):
                    real = both[0:8, lo * 128 : lo * 128 + 128]
                    turned = both[8:16, lo * 128 : lo * 128 + 128]
                    swapped = jnp.where(
                        odd, pltpu.roll(turned, 32, 1), -pltpu.roll(turned, 96, 1)
                    )
                    acc[pl.ds(half * 384 + pp * 24 + lo * 12 + i, 8, stride=48), :] = (
                        real + swapped
                    )

        each(12, step)

    phase_half(1 - core)
    a1 = remote(
        acc.at[pl.ds(pl.multiple_of((1 - core) * 384, 8), 384), :], ra1,
        a1s_sem.at[0], a1r_sem.at[0], y * 2 + (1 - core), pb,
    )
    a1.start()
    phase_half(core)

    def z_rows(src):
        return table.at[pl.ds(pl.multiple_of((x * 8 + src) * 16, 16), 16), :]

    def wait_u1z(d):
        src = (z + d + 1) % 8
        remote(z_rows(src), z_rows(src), u1zs.at[0], u1zr.at[src], re, x * 8 + src).wait_recv()

    each(7, wait_u1z)

    def x_rows(src):
        return table.at[pl.ds(pl.multiple_of(src * 128, 128), 128), :]

    def u1x(d):
        return remote(x_rows(x), x_rows(x), u1xs.at[d], u1xr.at[x], re, ((x + d + 1) % 4) * 8 + z)

    each(3, lambda d: u1x(d).start())

    a1.wait_recv()
    mine = pl.multiple_of(core * 384, 8)
    ra1[...] = ra1[...] + acc[pl.ds(mine, 384), :]

    def block(ref, index):
        return ref.at[pl.ds(pl.multiple_of(index * 48, 8), 48), :]

    def a2(d):
        to = (y + d + 1) % 8
        return remote(block(ra1, to), block(ra2, y), a2s_sem.at[d], a2r_sem.at[y], to * 2 + core, pb)

    each(7, lambda d: a2(d).start())

    def wait_u1x(d):
        src = (x + d + 1) % 4
        remote(x_rows(src), x_rows(src), u1xs.at[0], u1xr.at[src], re, src * 8 + z).wait_recv()

    each(3, wait_u1x)

    for k in range(8):
        index = ((kco[0, k] & 7) * 8 + (kco[1, k] & 7)) * 8 + (kco[2, k] & 7)
        sel[k : k + 1, :] = table[pl.ds(index, 1), :]

    def choose(i):
        k, q = i // 4, pb * 4 + i % 4
        index = (
            ((kco[0, k] + qco[0, q]) & 7) * 8 + ((kco[1, k] + qco[1, q]) & 7)
        ) * 8 + ((kco[2, k] + qco[2, q]) & 7)
        sel[pl.ds(8 + i, 1), :] = table[pl.ds(index, 1), :]

    each(32, choose)

    def k_block(src):
        return usk.at[pl.ds(pl.multiple_of(src * 8, 8), 8), :]

    def q_block(src):
        return usq.at[pl.ds(pl.multiple_of(src * 32, 8), 32), :]

    def uk(d):
        return remote(sel.at[0:8, :], k_block(re), uks.at[d], ukr.at[re], (re + d + 1) % 16, pb)

    def uq(d):
        to = ((y + d + 1) % 8) * 2 + core
        return remote(sel.at[8:40, :], q_block(re), uqs.at[d], uqr.at[y], to, pb)

    each(15, lambda d: uk(d).start())
    each(7, lambda d: uq(d).start())
    usk[pl.ds(pl.multiple_of(re * 8, 8), 8), :] = sel[0:8, :]
    usq[pl.ds(pl.multiple_of(re * 32, 8), 32), :] = sel[8:40, :]

    def uf(i):
        src = i * 2 + core
        return remote(q_block(src), q_block(src), ufs.at[i], ufr.at[i], y * 2 + (1 - core), pb)

    lane12 = iota((12, 128), 1)
    permute_row = iota((96, 128), 0)
    block24 = (
        (permute_row >= 24).astype(i32)
        + (permute_row >= 48).astype(i32)
        + (permute_row >= 72).astype(i32)
    )
    rest = permute_row - 24 * block24
    part = (rest >= 12).astype(i32)
    target = part * 48 + 4 * (rest - 12 * part) + block24
    permute = (iota((96, 128), 1) == target).astype(f32).astype(bf16)

    def mode_q(q):
        v = [modes[pl.ds(tt * 4 + q, 12, stride=12), :] for tt in range(3)]
        r0, r1, r2 = pltpu.roll(v[0], 32, 1), pltpu.roll(v[1], 32, 1), pltpu.roll(v[1], 64, 1)
        r3, r4 = pltpu.roll(v[2], 64, 1), pltpu.roll(v[2], 96, 1)
        raw = [
            v[0],
            jnp.where(lane12 < 32, r0, r1),
            jnp.where(lane12 < 64, r2, r3),
            r4,
        ]
        plain, crossed = [], []
        for value in raw:
            value = jnp.where(lane12 < 96, value, 0.0)
            other = jnp.where(lane12 < 48, -pltpu.roll(value, 80, 1), pltpu.roll(value, 48, 1))
            plain.append(value)
            crossed.append(jnp.where(lane12 < 96, other, 0.0))
        point = pb * 4 + q
        for p in range(4):
            turn = (
                qco[0, point] * pcell[0, p]
                + qco[1, point] * pcell[1, p]
                + qco[2, point] * pcell[2, p]
            ) & 7
            cos_p, sin_p = wave(jnp.full((1, 128), turn, i32), 8)
            for a2 in range(2):
                for lo in range(2):
                    i = 2 * lo + a2
                    base = a2 * 192 + p * 24 + lo * 12
                    fq[base : base + 12, :] = cos_p * plain[i] + sin_p * crossed[i]
                    fq[base + 96 : base + 108, :] = cos_p * crossed[i] - sin_p * plain[i]
        high, low = split(fq[...])
        where = pl.ds(pl.multiple_of(q * 96, 96), 96)
        fh[where, :] = dot(permute, high, NT).astype(bf16)
        fl[where, :] = dot(permute, low, NT).astype(bf16)

    each(4, mode_q)

    def wait_uk(d):
        src = (re + d + 1) % 16
        remote(k_block(src), k_block(src), uks.at[0], ukr.at[src], src, pb).wait_recv()

    each(15, wait_uk)
    turned = unfold(usk[pl.ds(y, 16, stride=8), :], wide)
    real, imag = turned[0:32], turned[32:64]
    group = iota((32, 128), 1) >> 5
    pieces = []
    for a in range(2):
        pieces.append(jnp.where(group == 2 * a, real, jnp.where(group == 2 * a + 1, imag, 0.0)))
        pieces.append(jnp.where(group == 2 * a, -imag, jnp.where(group == 2 * a + 1, real, 0.0)))
    rotation = split(jnp.concatenate(pieces, axis=0))

    def wait_a2(d):
        src = (y + d + 1) % 8
        remote(block(ra2, src), block(ra2, src), a2s_sem.at[0], a2r_sem.at[src], re, pb).wait_recv()

    each(7, wait_a2)
    ra2[pl.ds(pl.multiple_of(y * 48, 8), 48), :] = ra1[pl.ds(pl.multiple_of(y * 48, 8), 48), :]
    total = ra2[0:48, :]
    for source in range(1, 8):
        total = total + ra2[source * 48 : source * 48 + 48, :]
    gkpad[...] = jnp.zeros_like(gkpad)
    gkpad[pl.ds(pl.multiple_of(core * 48, 8), 48), :] = total
    rotated = dot3(split(gkpad[...]), rotation, NN).T
    for ac in range(4):
        a3s[pl.ds(ac, 32, stride=4), :] = rotated[ac * 32 : ac * 32 + 32]

    def tile(ref, index):
        return ref.at[pl.ds(pl.multiple_of(index * 8, 8), 8), :]

    def a3(d):
        to = (re + d + 1) % 16
        return remote(tile(a3s, to), tile(a3r, re), a3s_sem.at[d], a3r_sem.at[re], to, pb)

    each(15, lambda d: a3(d).start())
    own_tile = pl.ds(pl.multiple_of(re * 8, 8), 8)
    a3r[own_tile, :] = a3s[own_tile, :]

    def wait_a3(d):
        src = (re + d + 1) % 16
        remote(tile(a3r, src), tile(a3r, src), a3s_sem.at[0], a3r_sem.at[src], src, pb).wait_recv()

    each(15, wait_a3)

    lane8 = iota((8, 128), 1)
    home = pl.multiple_of(pb * 48, 8)
    for n in range(2):
        v = [
            a3r[pl.ds(n * 4 + ac, 8, stride=16), :] + a3r[pl.ds(8 + n * 4 + ac, 8, stride=16), :]
            for ac in range(4)
        ]
        r1, r2, r3 = pltpu.roll(v[1], 96, 1), pltpu.roll(v[2], 64, 1), pltpu.roll(v[3], 32, 1)
        thirds = [
            jnp.where(lane8 < 96, v[0], r1),
            jnp.where(lane8 < 64, r1, r2),
            jnp.where(lane8 < 32, r2, r3),
        ]
        for t in range(3):
            for kh in range(2):
                xs[pl.ds(home + kh * 24 + t * 8 + n * 4, 4), :] = thirds[t][kh * 4 : kh * 4 + 4]

    def chunk(src, kh):
        return xs.at[pl.ds(pl.multiple_of(src * 48 + kh * 24, 8), 24), :]

    def bx(kh, zs, d):
        src = x * 8 + zs
        return remote(
            chunk(src, kh), chunk(src, kh), bxs.at[kh * 24 + zs * 3 + d], bxr.at[kh * 32 + src],
            re, ((x + d + 1) % 4) * 8 + z,
        )

    def bz(kh, d):
        return remote(
            chunk(pb, kh), chunk(pb, kh), bzs.at[kh * 7 + d], bzr.at[kh * 8 + z],
            re, x * 8 + (z + d + 1) % 8,
        )

    for kh in range(2):
        each(3, lambda d: bx(kh, z, d).start())
        each(7, lambda d: bz(kh, d).start())

    for kh in range(2):
        def pass_on(d):
            zs = (z + d + 1) % 8
            here = chunk(x * 8 + zs, kh)
            remote(here, here, bzs.at[0], bzr.at[kh * 8 + zs], re, pb).wait_recv()
            each(3, lambda e: bx(kh, zs, e).start())

        each(7, pass_on)

    uf_own = uf(y)
    uf_own.start()

    def wait_uq(d):
        src = (y + d + 1) % 8
        here = q_block(src * 2 + core)
        remote(here, here, uqs.at[0], uqr.at[src], re, pb).wait_recv()
        uf(src).start()

    each(7, wait_uq)

    def wait_uf(i):
        here = q_block(i * 2 + (1 - core))
        remote(here, here, ufs.at[0], ufr.at[i], re, pb).wait_recv()

    each(8, wait_uf)

    def pair_matrix(i):
        kk, q = i // 4, i % 4
        for kl in range(2):
            value = unfold(usq[pl.ds((2 * kk + kl) * 4 + q, 16, stride=32), :], wide)
            for part in range(2):
                for n in range(2):
                    kept = jnp.where(
                        group == 2 * kl + n, value[part * 32 : part * 32 + 32], 0.0
                    )
                    high, low = split(kept)
                    base = pl.multiple_of(i * 256 + part * 128 + kl * 64 + n * 32, 32)
                    bh[pl.ds(base, 32), :] = high
                    bl[pl.ds(base, 32), :] = low

    each(16, pair_matrix)

    group24 = iota((24, 128), 1) >> 5
    row96 = iota((96, 128), 0)
    first = (
        (row96 < 12)
        | ((row96 >= 24) & (row96 < 36))
        | ((row96 >= 48) & (row96 < 60))
        | ((row96 >= 72) & (row96 < 84))
    )
    for kh in range(2):
        def wait_bx(i):
            src = ((x + i // 8 + 1) % 4) * 8 + i % 8
            here = chunk(src, kh)
            remote(here, here, bxs.at[0], bxr.at[kh * 32 + src], re, pb).wait_recv()

        each(24, wait_bx)

        for k4 in range(4):
            for n in range(2):
                for t in range(3):
                    high, low = split(xs[pl.ds(kh * 24 + t * 8 + n * 4 + k4, 32, stride=48), :])
                    to = k4 * 64 + n * 32
                    xh[to : to + 32, t * 128 : t * 128 + 128] = high
                    xl[to : to + 32, t * 128 : t * 128 + 128] = low
        result = dot3((fh[...], fl[...]), (xh[...], xl[...]), NT)
        ys[0:384, :] = result[:, 0:128]
        ys[384:768, :] = result[:, 128:256]

        def finish(i):
            kk, q = i // 4, i % 4
            value = ys[pl.ds(pl.multiple_of(kk * 384 + q * 96, 8), 96), :]
            other = jnp.where(first, pltpu.roll(value, 84, 0), -pltpu.roll(value, 12, 0))
            left = split(jnp.concatenate([value, other], axis=1))
            where = pl.ds(pl.multiple_of(((kh * 2 + kk) * 4 + q) * 256, 256), 256)
            res = dot3(left, (bh[where, :], bl[where, :]), NN)
            quarter = [res[j * 24 : j * 24 + 24] for j in range(4)]
            for kl in range(2):
                for n in range(2):
                    to = 2 * kl + n
                    mixed = quarter[to]
                    for j in range(4):
                        if j != to:
                            shift = 32 * ((j - to) % 4)
                            mixed = jnp.where(
                                group24 == j, pltpu.roll(quarter[j], shift, 1), mixed
                            )
                    k = kh * 4 + kk * 2 + kl
                    out[pl.ds((k * 4 + q) * 48 + n, 24, stride=2), :] = mixed

        each(8, finish)

    each(7, lambda d: u1z(d).wait_send())
    each(3, lambda d: u1x(d).wait_send())
    a1.wait_send()
    each(7, lambda d: a2(d).wait_send())
    each(15, lambda d: uk(d).wait_send())
    each(7, lambda d: uq(d).wait_send())
    each(8, lambda d: uf(d).wait_send())
    each(15, lambda d: a3(d).wait_send())
    for kh in range(2):
        each(7, lambda d: bz(kh, d).wait_send())
        each(24, lambda i: bx(kh, i // 3, i % 3).wait_send())


def body(
    wannier_coupling,
    electron_cells,
    phonon_cells,
    kpoint_coords,
    qpoint_coords,
    band_rotations,
    mode_vectors,
):
    smem = pl.BlockSpec(memory_space=pltpu.SMEM)
    vmem = pl.BlockSpec(memory_space=pltpu.VMEM)
    hbm = pl.BlockSpec(memory_space=pl.ANY)
    V, D = pltpu.VMEM, pltpu.SemaphoreType.DMA
    result = pl.pallas_call(
        kernel,
        out_shape=jax.ShapeDtypeStruct((1536, 128), f32),
        in_specs=[hbm, vmem, smem, smem, smem, hbm, vmem],
        out_specs=vmem,
        scratch_shapes=[
            V((3072, 128), f32),
            V((768, 128), f32),
            V((384, 128), f32),
            V((384, 128), f32),
            V((512, 128), f32),
            V((40, 128), f32),
            V((128, 128), f32),
            V((512, 128), f32),
            V((64, 128), f32),
            V((128, 128), f32),
            V((128, 128), f32),
            V((128, 128), f32),
            V((1536, 128), f32),
            V((384, 128), f32),
            V((384, 384), bf16),
            V((384, 384), bf16),
            V((4096, 128), bf16),
            V((4096, 128), bf16),
            V((256, 384), bf16),
            V((256, 384), bf16),
            V((768, 128), f32),
            D((1,)), D((1,)), D((7,)), D((8,)), D((3,)), D((4,)), D((1,)), D((1,)),
            D((7,)), D((8,)), D((15,)), D((16,)), D((7,)), D((8,)), D((8,)), D((8,)),
            D((15,)), D((16,)), D((14,)), D((16,)), D((48,)), D((64,)),
        ],
        compiler_params=pltpu.CompilerParams(
            collective_id=0, has_side_effects=True, vmem_limit_bytes=40 * 1024 * 1024
        ),
        name="interpolate",
    )(
        wannier_coupling.reshape(3072, 128),
        electron_cells,
        phonon_cells,
        kpoint_coords,
        qpoint_coords,
        band_rotations,
        mode_vectors.reshape(4, 36, 128).transpose(1, 0, 2).reshape(144, 128),
    )
    return result.reshape(8, 4, 24, 2, 128).transpose(0, 1, 3, 2, 4).reshape(8, 4, 2, 3072)


def solution(mesh):
    return jax.shard_map(
        body,
        mesh=mesh,
        in_specs=(
            P("re", None, "pb", None),
            P(None, "re"),
            P(),
            P(),
            P(),
            P("pb", None),
            P("pb", None),
        ),
        out_specs=P(None, "pb", "re", None),
        check_vma=False,
    )
```

profile of v0, /device:TPU:1, one launch (start us, length us, event | category | flops | bytes accessed | tf_op | source)
XLA Modules:
  0.0 68.9 jit_solution(11289560202857730078)
XLA Ops:
  0.0 0.9 %reshape.16 = f32[4,36,128]{2,1,0:T(8,128)S(1)} reshape(f32[4,4608]{1,0:T(4,128)} %param.13) | data formatting | bytes 147456 | tf_op jit(solution)/shard_map/reshape | solution.py:527
  0.9 0.0 copy-start
  1.0 1.4 %copy-done = f32[32,4,1,3072]{3,2,1,0:T(1,128)S(1)} copy-done((f32[32,4,1,3072]{3,2,1,0:T(1,128)S(1)}, f32[32,4,1,3072]{3,2,1,0:T(1,128)}, u32[]{:S(2)}) %copy-start) | copy-done | bytes 1572888
  2.4 0.0 copy-start.1
  2.4 0.9 %copy-done.1 = f32[16,2048]{1,0:T(8,128)S(1)} copy-done((f32[16,2048]{1,0:T(8,128)S(1)}, f32[16,2048]{1,0:T(8,128)}, u32[]{:S(2)}) %copy-start.1) | copy-done | bytes 131096
  3.3 0.0 copy-start.2
  3.3 0.7 copy-done.2
  3.9 0.0 copy-start.3
  3.9 0.7 copy-done.3
  4.6 0.0 copy-start.4
  4.6 0.7 copy-done.4
  5.3 0.0 copy-start.5
  5.3 0.7 copy-done.5
  6.0 62.0 %interpolate.1 = f32[1536,128]{1,0:T(8,128)S(1)} custom-call(f32[3072,128]{1,0:T(8,128)S(1)} %bitcast.9, s32[3,32]{1,0:T(4,128)S(1)} %copy-done.2, s32[3,4]{1,0:T(4,128)S(1)} %copy-done.3, s32[3,8]{1,0:T(4,128)S(1)} %copy-done.4, s32[3,128]{1,0:T(4,128)S(1)} %copy-done.5, f32[16,2048]{1,0:T(8,128)S(1)} %copy-done.1, f32[144,128]{1,0:T(8,128)S(1)} %bitcast.10), custom_call_target="tpu_custom_call" | custom-call | tf_op jit(solution)/shard_map/interpolate/pallas_call | solution.py:485
  68.0 0.9 %copy.13 = f32[8,4,2,3072]{3,2,1,0:T(2,128)} copy(f32[8,4,2,3072]{3,2,1,0:T(2,128)S(1)} %bitcast.8) | data formatting | bytes 1572864
  (1 shorter events, 0.0 us)
Async XLA Ops:
  0.9 1.4 %copy-start = (f32[32,4,1,3072]{3,2,1,0:T(1,128)S(1)}, f32[32,4,1,3072]{3,2,1,0:T(1,128)}, u32[]{:S(2)}) copy-start(f32[32,4,1,3072]{3,2,1,0:T(1,128)} %param.7) | copy-start | bytes 4718596
  2.4 0.9 %copy-start.1 = (f32[16,2048]{1,0:T(8,128)S(1)}, f32[16,2048]{1,0:T(8,128)}, u32[]{:S(2)}) copy-start(f32[16,2048]{1,0:T(8,128)} %rot_hbm.1) | copy-start | bytes 393220
  3.3 0.7 copy-start.2
  3.9 0.7 copy-start.3
  4.6 0.7 copy-start.4
  5.3 0.7 copy-start.5
where the time goes:
time: 69.2 us; the launch traced here: 68.9 us
  Pallas kernels  62 us (90%)
  local copies, waits for them, and re-layouts  6.85 us (10%)
    pallas_call x1, Pallas kernels, body(): pl.pallas_call(kernel, out_shape=jax.ShapeDtypeStruct((1536, 128), f32),...  62 us
    unnamed x13, local copies, waits for them, and re-layouts  5.91 us

commit v1 on v0

--- a/solution.py
+++ b/solution.py
@@ -9,6 +9,9 @@
 
 f32, bf16, i32 = jnp.float32, jnp.bfloat16, jnp.int32
 MESH = pl.DeviceIdType.MESH
+NEAR = (0, 6, 1, 5, 2, 4, 3)
+NEAR_X = (0, 2, 1)
+NEAR_RE = (0, 14, 1, 13, 2, 12, 3, 11, 4, 10, 5, 9, 6, 8, 7)
 NN = ((1,), (0,))
 NT = ((1,), (1,))
 
@@ -43,21 +46,21 @@
     return cosine, sine
 
 
-def unfold(slices, wide):
+def unfold(slices, wide, region):
     group = iota((16, 128), 1) >> 5
     for j in range(4):
-        wide[pl.ds(j, 16, stride=4), :] = jnp.where(group == j, slices, 0.0)
-    kept = wide[...]
+        wide[pl.ds(region * 64 + j, 16, stride=4), :] = jnp.where(group == j, slices, 0.0)
+    kept = wide[region * 64 : region * 64 + 64, :]
     kept = kept + pltpu.roll(kept, 64, 1)
     return kept + pltpu.roll(kept, 32, 1)
 
 
 def kernel(
-    g_hbm, cells, pcell, kco, qco, rot_hbm, modes, out,
-    g, acc, ra1, ra2, table, sel, usk, usq, wide, gkpad, a3s, a3r, xs,
-    fq, fh, fl, bh, bl, xh, xl, ys,
-    gsem, tsem, u1zs, u1zr, u1xs, u1xr, a1s_sem, a1r_sem, a2s_sem, a2r_sem,
-    uks, ukr, uqs, uqr, ufs, ufr, a3s_sem, a3r_sem, bzs, bzr, bxs, bxr,
+    g_hbm, cells_hbm, pcell_hbm, kco_hbm, qco_hbm, rot_hbm, modes_hbm, out,
+    cells, pcell, kco, qco, flat, modes, rot, g, acc, ra1, ra2, table, sel, kz, kx, usq, wide,
+    gkpad, a3s, a3r, xs, fq, fh, fl, bh, bl, xh, xl, ys,
+    gsem, rotsem, insem, u1zs, u1zr, u1xs, u1xr, a1s_sem, a1r_sem, a2s_sem, a2r_sem,
+    kzs, kzr, kxs, kxr, uqs, uqr, ufs, ufr, a3s_sem, a3r_sem, bzs, bzr, bxs, bxr,
 ):
     re = lax.axis_index("re")
     pb = lax.axis_index("pb")
@@ -77,13 +80,28 @@
 
         lax.fori_loop(0, count, step, 0)
 
+    small = [
+        pltpu.make_async_copy(src, dst, insem.at[i])
+        for i, (src, dst) in enumerate(
+            [(kco_hbm, kco), (cells_hbm, cells), (pcell_hbm, pcell), (qco_hbm, qco)]
+        )
+    ]
+    modes_copy = pltpu.make_async_copy(modes_hbm, flat, insem.at[4])
+
+    def rot_copy(i):
+        return pltpu.make_async_copy(
+            rot_hbm.at[:, pl.ds(pl.multiple_of(i * 128, 128), 128)],
+            rot.at[pl.ds(pl.multiple_of(i * 16, 16), 16), :],
+            rotsem.at[i],
+        )
+
+    for copy in small:
+        copy.start()
     g_copy = pltpu.make_async_copy(g_hbm, g, gsem.at[0])
     g_copy.start()
+    each(16, lambda i: rot_copy(i).start())
     own_rows = table.at[pl.ds(pl.multiple_of(pb * 16, 16), 16), :]
-    t_copy = pltpu.make_async_copy(
-        rot_hbm.at[:, pl.ds(pl.multiple_of(re * 128, 128), 128)], own_rows, tsem.at[0]
-    )
-    t_copy.start()
+    modes_copy.start()
 
     barrier = pltpu.get_barrier_semaphore()
 
@@ -100,66 +118,118 @@
             barrier, 1, device_id=(re, ((x + d + 1) % 4) * 8 + z), device_id_type=MESH
         )
 
-    each(15, greet_re)
-    each(7, greet_z)
+    for d in NEAR_RE[::-1]:
+        greet_re(d)
+    for d in NEAR[::-1]:
+        greet_z(d)
     each(3, greet_x)
-
-    row = iota((8, 32), 0)
-    turns = jnp.zeros((8, 32), i32)
+    for copy in small:
+        copy.wait()
+
+    row = iota((8, 64), 0)
+    turns = jnp.zeros((8, 64), i32)
+    twice = jnp.concatenate([cells[...], cells[...]], axis=1)
     for d in range(3):
-        coef = jnp.zeros((8, 32), i32)
+        coef = jnp.zeros((8, 64), i32)
         for k in range(8):
             coef = jnp.where(row == k, 2 * kco[d, k] + 1, coef)
-        turns = turns + coef * jnp.broadcast_to(cells[d : d + 1, :], (8, 32))
+        turns = turns + coef * jnp.broadcast_to(twice[d : d + 1, :], (8, 64))
     cosine, sine = wave(turns & 15, 16)
-    waves_h, waves_l = split(jnp.concatenate([cosine, sine], axis=0))
-    waves = jnp.concatenate([waves_h, waves_l], axis=0)
-
+    waves = jnp.concatenate(split(jnp.concatenate([cosine, sine], axis=0)), axis=0)
+
+    k_index = ((kco[0, y] & 7) * 8 + (kco[1, y] & 7)) * 8 + (kco[2, y] & 7)
+    each(16, lambda i: rot_copy(i).wait())
+    held = jnp.full((16, 128), k_index >> 4, i32) == jnp.full((16, 128), pb, i32)
+
+    def kz_block(src):
+        return kz.at[pl.ds(pl.multiple_of(src * 16, 16), 16), :]
+
+    def kx_block(src):
+        return kx.at[pl.ds(pl.multiple_of(src * 16, 16), 16), :]
+
+    kz[pl.ds(pl.multiple_of(z * 16, 16), 16), :] = jnp.where(
+        held, rot[pl.ds(k_index & 15, 16, stride=16), :], 0.0
+    )
+    own_rows[...] = rot[pl.ds(pl.multiple_of(re * 16, 16), 16), :]
+
+    odd = ((iota((8, 128), 1) >> 5) & 1) == 1
+
+    def phase_part(half, pp):
+        for i in range(12):
+            highs, lows = [], []
+            for lo in range(2):
+                start = half * 48 + pp * 24 + 2 * i + lo
+                high, low = split(g[pl.ds(start, 32, stride=96), :])
+                highs.append(high)
+                lows.append(low)
+            stacked = jnp.concatenate(
+                [jnp.concatenate(highs, axis=1), jnp.concatenate(lows, axis=1)], axis=0
+            )
+            both = dot(waves, stacked, NN)
+            both = both[0:16] + both[16:32]
+            for lo in range(2):
+                real = both[0:8, lo * 128 : lo * 128 + 128]
+                turned = both[8:16, lo * 128 : lo * 128 + 128]
+                swapped = jnp.where(odd, pltpu.roll(turned, 32, 1), -pltpu.roll(turned, 96, 1))
+                acc[pl.ds(half * 384 + pp * 24 + lo * 12 + i, 8, stride=48), :] = real + swapped
+
+    g_copy.wait()
+    for pp in range(2):
+        phase_part(1 - core, pp)
     pl.semaphore_wait(barrier, 25)
-    t_copy.wait()
-
-    def u1z(d):
-        return remote(
-            own_rows, own_rows, u1zs.at[d], u1zr.at[z], re, x * 8 + (z + d + 1) % 8
-        )
-
-    each(7, lambda d: u1z(d).start())
-    g_copy.wait()
-
-    odd = ((iota((8, 128), 1) >> 5) & 1) == 1
-
-    def phase_half(half):
-        def step(i):
-            for pp in range(2):
-                highs, lows = [], []
-                for lo in range(2):
-                    start = half * 48 + pp * 24 + 2 * i + lo
-                    high, low = split(g[pl.ds(start, 32, stride=96), :])
-                    highs.append(high)
-                    lows.append(low)
-                high = jnp.concatenate(highs, axis=1)
-                low = jnp.concatenate(lows, axis=1)
-                first = dot(waves, high, NN)
-                both = first[0:16] + first[16:32] + dot(waves_h, low, NN)
-                for lo in range(2):
-                    real = both[0:8, lo * 128 : lo * 128 + 128]
-                    turned = both[8:16, lo * 128 : lo * 128 + 128]
-                    swapped = jnp.where(
-                        odd, pltpu.roll(turned, 32, 1), -pltpu.roll(turned, 96, 1)
-                    )
-                    acc[pl.ds(half * 384 + pp * 24 + lo * 12 + i, 8, stride=48), :] = (
-                        real + swapped
-                    )
-
-        each(12, step)
-
-    phase_half(1 - core)
     a1 = remote(
         acc.at[pl.ds(pl.multiple_of((1 - core) * 384, 8), 384), :], ra1,
         a1s_sem.at[0], a1r_sem.at[0], y * 2 + (1 - core), pb,
     )
     a1.start()
-    phase_half(core)
+
+    def kz_copy(d):
+        return remote(
+            kz_block(z), kz_block(z), kzs.at[d], kzr.at[z], re, x * 8 + (z + d + 1) % 8
+        )
+
+    def u1z(d):
+        return remote(
+            own_rows, own_rows, u1zs.at[d], u1zr.at[z], re, x * 8 + (z + d + 1) % 8
+        )
+
+    for d in NEAR:
+        kz_copy(d).start()
+    for d in NEAR:
+        u1z(d).start()
+    for pp in range(2):
+        phase_part(core, pp)
+
+    a1.wait_recv()
+    mine = pl.multiple_of(core * 384, 8)
+    ra1[...] = ra1[...] + acc[pl.ds(mine, 384), :]
+
+    def block(ref, index):
+        return ref.at[pl.ds(pl.multiple_of(index * 48, 8), 48), :]
+
+    def a2(d):
+        to = (y + d + 1) % 8
+        return remote(block(ra1, to), block(ra2, y), a2s_sem.at[d], a2r_sem.at[y], to * 2 + core, pb)
+
+    for d in NEAR:
+        a2(d).start()
+
+    def wait_kz(d):
+        src = (z + d + 1) % 8
+        remote(kz_block(src), kz_block(src), kzs.at[0], kzr.at[src], re, pb).wait_recv()
+
+    each(7, wait_kz)
+    found = kz[0:16, :]
+    for s in range(1, 8):
+        found = found + kz[s * 16 : s * 16 + 16, :]
+    kx[pl.ds(pl.multiple_of(x * 16, 16), 16), :] = found
+
+    def kx_copy(d):
+        return remote(
+            kx_block(x), kx_block(x), kxs.at[d], kxr.at[x], re, ((x + d + 1) % 4) * 8 + z
+        )
+
+    each(3, lambda d: kx_copy(d).start())
 
     def z_rows(src):
         return table.at[pl.ds(pl.multiple_of((x * 8 + src) * 16, 16), 16), :]
@@ -178,60 +248,11 @@
 
     each(3, lambda d: u1x(d).start())
 
-    a1.wait_recv()
-    mine = pl.multiple_of(core * 384, 8)
-    ra1[...] = ra1[...] + acc[pl.ds(mine, 384), :]
-
-    def block(ref, index):
-        return ref.at[pl.ds(pl.multiple_of(index * 48, 8), 48), :]
-
-    def a2(d):
-        to = (y + d + 1) % 8
-        return remote(block(ra1, to), block(ra2, y), a2s_sem.at[d], a2r_sem.at[y], to * 2 + core, pb)
-
-    each(7, lambda d: a2(d).start())
-
-    def wait_u1x(d):
-        src = (x + d + 1) % 4
-        remote(x_rows(src), x_rows(src), u1xs.at[0], u1xr.at[src], re, src * 8 + z).wait_recv()
-
-    each(3, wait_u1x)
-
-    for k in range(8):
-        index = ((kco[0, k] & 7) * 8 + (kco[1, k] & 7)) * 8 + (kco[2, k] & 7)
-        sel[k : k + 1, :] = table[pl.ds(index, 1), :]
-
-    def choose(i):
-        k, q = i // 4, pb * 4 + i % 4
-        index = (
-            ((kco[0, k] + qco[0, q]) & 7) * 8 + ((kco[1, k] + qco[1, q]) & 7)
-        ) * 8 + ((kco[2, k] + qco[2, q]) & 7)
-        sel[pl.ds(8 + i, 1), :] = table[pl.ds(index, 1), :]
-
-    each(32, choose)
-
-    def k_block(src):
-        return usk.at[pl.ds(pl.multiple_of(src * 8, 8), 8), :]
-
-    def q_block(src):
-        return usq.at[pl.ds(pl.multiple_of(src * 32, 8), 32), :]
-
-    def uk(d):
-        return remote(sel.at[0:8, :], k_block(re), uks.at[d], ukr.at[re], (re + d + 1) % 16, pb)
-
-    def uq(d):
-        to = ((y + d + 1) % 8) * 2 + core
-        return remote(sel.at[8:40, :], q_block(re), uqs.at[d], uqr.at[y], to, pb)
-
-    each(15, lambda d: uk(d).start())
-    each(7, lambda d: uq(d).start())
-    usk[pl.ds(pl.multiple_of(re * 8, 8), 8), :] = sel[0:8, :]
-    usq[pl.ds(pl.multiple_of(re * 32, 8), 32), :] = sel[8:40, :]
-
-    def uf(i):
-        src = i * 2 + core
-        return remote(q_block(src), q_block(src), ufs.at[i], ufr.at[i], y * 2 + (1 - core), pb)
-
+    modes_copy.wait()
+    for tile_index in range(36):
+        modes[tile_index * 4 : tile_index * 4 + 4, :] = flat[
+            :, tile_index * 128 : tile_index * 128 + 128
+        ]
     lane12 = iota((12, 128), 1)
     permute_row = iota((96, 128), 0)
     block24 = (
@@ -281,12 +302,13 @@
 
     each(4, mode_q)
 
-    def wait_uk(d):
-        src = (re + d + 1) % 16
-        remote(k_block(src), k_block(src), uks.at[0], ukr.at[src], src, pb).wait_recv()
-
-    each(15, wait_uk)
-    turned = unfold(usk[pl.ds(y, 16, stride=8), :], wide)
+    def wait_kx(d):
+        src = (x + d + 1) % 4
+        remote(kx_block(src), kx_block(src), kxs.at[0], kxr.at[src], re, pb).wait_recv()
+
+    each(3, wait_kx)
+    k_row = kx[0:16, :] + kx[16:32, :] + kx[32:48, :] + kx[48:64, :]
+    turned = unfold(k_row, wide, 0)
     real, imag = turned[0:32], turned[32:64]
     group = iota((32, 128), 1) >> 5
     pieces = []
@@ -317,9 +339,40 @@
         to = (re + d + 1) % 16
         return remote(tile(a3s, to), tile(a3r, re), a3s_sem.at[d], a3r_sem.at[re], to, pb)
 
-    each(15, lambda d: a3(d).start())
+    for d in NEAR_RE:
+        a3(d).start()
     own_tile = pl.ds(pl.multiple_of(re * 8, 8), 8)
     a3r[own_tile, :] = a3s[own_tile, :]
+
+    def wait_u1x(d):
+        src = (x + d + 1) % 4
+        remote(x_rows(src), x_rows(src), u1xs.at[0], u1xr.at[src], re, src * 8 + z).wait_recv()
+
+    each(3, wait_u1x)
+
+    def choose(i):
+        k, q = i // 4, pb * 4 + i % 4
+        index = (
+            ((kco[0, k] + qco[0, q]) & 7) * 8 + ((kco[1, k] + qco[1, q]) & 7)
+        ) * 8 + ((kco[2, k] + qco[2, q]) & 7)
+        sel[pl.ds(i, 1), :] = table[pl.ds(index, 1), :]
+
+    each(32, choose)
+
+    def q_block(src):
+        return usq.at[pl.ds(pl.multiple_of(src * 32, 8), 32), :]
+
+    def uq(d):
+        to = ((y + d + 1) % 8) * 2 + core
+        return remote(sel, q_block(re), uqs.at[d], uqr.at[y], to, pb)
+
+    for d in NEAR:
+        uq(d).start()
+    usq[pl.ds(pl.multiple_of(re * 32, 8), 32), :] = sel[...]
+
+    def uf(i):
+        src = i * 2 + core
+        return remote(q_block(src), q_block(src), ufs.at[i], ufr.at[i], y * 2 + (1 - core), pb)
 
     def wait_a3(d):
         src = (re + d + 1) % 16
@@ -361,17 +414,21 @@
         )
 
     for kh in range(2):
-        each(3, lambda d: bx(kh, z, d).start())
-        each(7, lambda d: bz(kh, d).start())
+        for d in NEAR:
+            bz(kh, d).start()
+        for d in NEAR_X:
+            bx(kh, z, d).start()
 
     for kh in range(2):
         def pass_on(d):
             zs = (z + d + 1) % 8
             here = chunk(x * 8 + zs, kh)
             remote(here, here, bzs.at[0], bzr.at[kh * 8 + zs], re, pb).wait_recv()
-            each(3, lambda e: bx(kh, zs, e).start())
-
-        each(7, pass_on)
+            for e in NEAR_X:
+                bx(kh, zs, e).start()
+
+        for d in NEAR:
+            pass_on(d)
 
     uf_own = uf(y)
     uf_own.start()
@@ -382,7 +439,8 @@
         remote(here, here, uqs.at[0], uqr.at[src], re, pb).wait_recv()
         uf(src).start()
 
-    each(7, wait_uq)
+    for d in NEAR:
+        wait_uq(d)
 
     def wait_uf(i):
         here = q_block(i * 2 + (1 - core))
@@ -390,21 +448,25 @@
 
     each(8, wait_uf)
 
-    def pair_matrix(i):
-        kk, q = i // 4, i % 4
-        for kl in range(2):
-            value = unfold(usq[pl.ds((2 * kk + kl) * 4 + q, 16, stride=32), :], wide)
-            for part in range(2):
-                for n in range(2):
-                    kept = jnp.where(
-                        group == 2 * kl + n, value[part * 32 : part * 32 + 32], 0.0
-                    )
-                    high, low = split(kept)
-                    base = pl.multiple_of(i * 256 + part * 128 + kl * 64 + n * 32, 32)
-                    bh[pl.ds(base, 32), :] = high
-                    bl[pl.ds(base, 32), :] = low
-
-    each(16, pair_matrix)
+    def pair_matrices(kk):
+        for q in range(4):
+            for kl in range(2):
+                value = unfold(
+                    usq[pl.ds((2 * kk + kl) * 4 + q, 16, stride=32), :], wide, q * 2 + kl
+                )
+                for part in range(2):
+                    for n in range(2):
+                        kept = jnp.where(
+                            group == 2 * kl + n, value[part * 32 : part * 32 + 32], 0.0
+                        )
+                        high, low = split(kept)
+                        base = pl.multiple_of(
+                            (kk * 4 + q) * 256 + part * 128 + kl * 64 + n * 32, 32
+                        )
+                        bh[pl.ds(base, 32), :] = high
+                        bl[pl.ds(base, 32), :] = low
+
+    each(4, pair_matrices)
 
     group24 = iota((24, 128), 1) >> 5
     row96 = iota((96, 128), 0)
@@ -433,34 +495,35 @@
         ys[0:384, :] = result[:, 0:128]
         ys[384:768, :] = result[:, 128:256]
 
-        def finish(i):
-            kk, q = i // 4, i % 4
-            value = ys[pl.ds(pl.multiple_of(kk * 384 + q * 96, 8), 96), :]
-            other = jnp.where(first, pltpu.roll(value, 84, 0), -pltpu.roll(value, 12, 0))
-            left = split(jnp.concatenate([value, other], axis=1))
-            where = pl.ds(pl.multiple_of(((kh * 2 + kk) * 4 + q) * 256, 256), 256)
-            res = dot3(left, (bh[where, :], bl[where, :]), NN)
-            quarter = [res[j * 24 : j * 24 + 24] for j in range(4)]
-            for kl in range(2):
-                for n in range(2):
-                    to = 2 * kl + n
-                    mixed = quarter[to]
-                    for j in range(4):
-                        if j != to:
-                            shift = 32 * ((j - to) % 4)
-                            mixed = jnp.where(
-                                group24 == j, pltpu.roll(quarter[j], shift, 1), mixed
-                            )
-                    k = kh * 4 + kk * 2 + kl
-                    out[pl.ds((k * 4 + q) * 48 + n, 24, stride=2), :] = mixed
-
-        each(8, finish)
+        def finish(kk):
+            for q in range(4):
+                value = ys[pl.ds(pl.multiple_of(kk * 384 + q * 96, 8), 96), :]
+                other = jnp.where(first, pltpu.roll(value, 84, 0), -pltpu.roll(value, 12, 0))
+                left = split(jnp.concatenate([value, other], axis=1))
+                where = pl.ds(pl.multiple_of(((kh * 2 + kk) * 4 + q) * 256, 256), 256)
+                res = dot3(left, (bh[where, :], bl[where, :]), NN)
+                quarter = [res[j * 24 : j * 24 + 24] for j in range(4)]
+                for kl in range(2):
+                    for n in range(2):
+                        to = 2 * kl + n
+                        mixed = quarter[to]
+                        for j in range(4):
+                            if j != to:
+                                shift = 32 * ((j - to) % 4)
+                                mixed = jnp.where(
+                                    group24 == j, pltpu.roll(quarter[j], shift, 1), mixed
+                                )
+                        k = kh * 4 + kk * 2 + kl
+                        out[pl.ds((k * 4 + q) * 48 + n, 24, stride=2), :] = mixed
+
+        each(2, finish)
 
     each(7, lambda d: u1z(d).wait_send())
     each(3, lambda d: u1x(d).wait_send())
     a1.wait_send()
     each(7, lambda d: a2(d).wait_send())
-    each(15, lambda d: uk(d).wait_send())
+    each(7, lambda d: kz_copy(d).wait_send())
+    each(3, lambda d: kx_copy(d).wait_send())
     each(7, lambda d: uq(d).wait_send())
     each(8, lambda d: uf(d).wait_send())
     each(15, lambda d: a3(d).wait_send())
@@ -478,25 +541,32 @@
     band_rotations,
     mode_vectors,
 ):
-    smem = pl.BlockSpec(memory_space=pltpu.SMEM)
+    hbm = pl.BlockSpec(memory_space=pltpu.HBM)
     vmem = pl.BlockSpec(memory_space=pltpu.VMEM)
-    hbm = pl.BlockSpec(memory_space=pl.ANY)
-    V, D = pltpu.VMEM, pltpu.SemaphoreType.DMA
+    V, S, D = pltpu.VMEM, pltpu.SMEM, pltpu.SemaphoreType.DMA
     result = pl.pallas_call(
         kernel,
         out_shape=jax.ShapeDtypeStruct((1536, 128), f32),
-        in_specs=[hbm, vmem, smem, smem, smem, hbm, vmem],
+        in_specs=[hbm] * 7,
         out_specs=vmem,
         scratch_shapes=[
+            V((3, 32), i32),
+            S((3, 4), i32),
+            S((3, 8), i32),
+            S((3, 128), i32),
+            V((4, 4608), f32),
+            V((144, 128), f32),
+            V((256, 128), f32),
             V((3072, 128), f32),
             V((768, 128), f32),
             V((384, 128), f32),
             V((384, 128), f32),
             V((512, 128), f32),
-            V((40, 128), f32),
+            V((32, 128), f32),
             V((128, 128), f32),
+            V((64, 128), f32),
             V((512, 128), f32),
-            V((64, 128), f32),
+            V((512, 128), f32),
             V((128, 128), f32),
             V((128, 128), f32),
             V((128, 128), f32),
@@ -509,12 +579,14 @@
             V((256, 384), bf16),
             V((256, 384), bf16),
             V((768, 128), f32),
-            D((1,)), D((1,)), D((7,)), D((8,)), D((3,)), D((4,)), D((1,)), D((1,)),
-            D((7,)), D((8,)), D((15,)), D((16,)), D((7,)), D((8,)), D((8,)), D((8,)),
+            D((1,)), D((16,)), D((5,)),
+            D((7,)), D((8,)), D((3,)), D((4,)), D((1,)), D((1,)),
+            D((7,)), D((8,)),
+            D((7,)), D((8,)), D((3,)), D((4,)), D((7,)), D((8,)), D((8,)), D((8,)),
             D((15,)), D((16,)), D((14,)), D((16,)), D((48,)), D((64,)),
         ],
         compiler_params=pltpu.CompilerParams(
-            collective_id=0, has_side_effects=True, vmem_limit_bytes=40 * 1024 * 1024
+            collective_id=0, has_side_effects=True, vmem_limit_bytes=60 * 1024 * 1024
         ),
         name="interpolate",
     )(
@@ -524,7 +596,7 @@
         kpoint_coords,
         qpoint_coords,
         band_rotations,
-        mode_vectors.reshape(4, 36, 128).transpose(1, 0, 2).reshape(144, 128),
+        mode_vectors,
     )
     return result.reshape(8, 4, 24, 2, 128).transpose(0, 1, 3, 2, 4).reshape(8, 4, 2, 3072)
 

time: 69.2 us -> 51.4 us (0.74)
  Pallas kernels: 62 us -> 49.1 us
  local copies, waits for them, and re-layouts: 6.85 us -> 2.07 us
    pallas_call x1, Pallas kernels: 62 us -> 49.1 us  [body(): pl.pallas_call(kernel, out_shape=jax.ShapeDtypeStruct((1536, 128), f32),...]
    unnamed x13 -> x1, local copies, waits for them, and re-layouts: 5.91 us -> 2.07 us
    reshape x1 -> x0, local copies, waits for them, and re-layouts: 0.91 us -> none  [body(): mode_vectors.reshape(4, 36, 128).transpose(1, 0, 2).reshape(144, 128)]
where the time goes in v1:
time: 51.4 us; the launch traced here: 51.2 us
  Pallas kernels  49.1 us (96%)
  local copies, waits for them, and re-layouts  2.07 us (4%)
    pallas_call x1, Pallas kernels, body(): pl.pallas_call(kernel, out_shape=jax.ShapeDtypeStruct((1536, 128), f32),...  49.1 us
    unnamed x1, local copies, waits for them, and re-layouts  2.07 us

profile of v1, /device:TPU:1, one launch (start us, length us, event | category | flops | bytes accessed | tf_op | source)
XLA Modules:
  0.0 51.2 jit_solution(4289817073480682113)
XLA Ops:
  0.0 49.1 %interpolate.1 = f32[1536,128]{1,0:T(8,128)} custom-call(f32[3072,128]{1,0:T(8,128)} %bitcast.7, s32[3,32]{1,0:T(4,128)} %cells_hbm.1, s32[3,4]{1,0:T(4,128)} %pcell_hbm.1, s32[3,8]{1,0:T(4,128)} %kco_hbm.1, s32[3,128]{1,0:T(4,128)} %qco_hbm.1, f32[16,2048]{1,0:T(8,128)} %rot_hbm.1, f32[4,4608]{1,0:T(4,128)} %modes_hbm.1), custom_call_target="tpu_custom_call" | custom-call | tf_op jit(solution)/shard_map/interpolate/pallas_call | solution.py:547
  49.1 2.1 %copy.10 = f32[8,4,2,3072]{3,2,1,0:T(2,128)} copy(f32[8,4,2,3072]{3,2,1,0:T(2,128)} %bitcast.6) | data formatting | bytes 1572864

commit v2 on v1

--- a/solution.py
+++ b/solution.py
@@ -58,7 +58,7 @@
 def kernel(
     g_hbm, cells_hbm, pcell_hbm, kco_hbm, qco_hbm, rot_hbm, modes_hbm, out,
     cells, pcell, kco, qco, flat, modes, rot, g, acc, ra1, ra2, table, sel, kz, kx, usq, wide,
-    gkpad, a3s, a3r, xs, fq, fh, fl, bh, bl, xh, xl, ys,
+    a3s, a3r, xs, fq, fh, fl, bh, bl, xh, xl, ys,
     gsem, rotsem, insem, u1zs, u1zr, u1xs, u1xr, a1s_sem, a1r_sem, a2s_sem, a2r_sem,
     kzs, kzr, kxs, kxr, uqs, uqr, ufs, ufr, a3s_sem, a3r_sem, bzs, bzr, bxs, bxr,
 ):
@@ -80,6 +80,26 @@
 
         lax.fori_loop(0, count, step, 0)
 
+    barrier = pltpu.get_barrier_semaphore()
+
+    def greet_re(d):
+        pl.semaphore_signal(barrier, 1, device_id=((re + d + 1) % 16, pb), device_id_type=MESH)
+
+    def greet_z(d):
+        pl.semaphore_signal(
+            barrier, 1, device_id=(re, x * 8 + (z + d + 1) % 8), device_id_type=MESH
+        )
+
+    def greet_x(d):
+        pl.semaphore_signal(
+            barrier, 1, device_id=(re, ((x + d + 1) % 4) * 8 + z), device_id_type=MESH
+        )
+
+    for d in NEAR_RE[::-1]:
+        greet_re(d)
+    for d in NEAR[::-1]:
+        greet_z(d)
+    each(3, greet_x)
     small = [
         pltpu.make_async_copy(src, dst, insem.at[i])
         for i, (src, dst) in enumerate(
@@ -95,34 +115,14 @@
             rotsem.at[i],
         )
 
+    g_copy = pltpu.make_async_copy(g_hbm, g, gsem.at[0])
+    g_copy.start()
     for copy in small:
         copy.start()
-    g_copy = pltpu.make_async_copy(g_hbm, g, gsem.at[0])
-    g_copy.start()
     each(16, lambda i: rot_copy(i).start())
     own_rows = table.at[pl.ds(pl.multiple_of(pb * 16, 16), 16), :]
     modes_copy.start()
 
-    barrier = pltpu.get_barrier_semaphore()
-
-    def greet_re(d):
-        pl.semaphore_signal(barrier, 1, device_id=((re + d + 1) % 16, pb), device_id_type=MESH)
-
-    def greet_z(d):
-        pl.semaphore_signal(
-            barrier, 1, device_id=(re, x * 8 + (z + d + 1) % 8), device_id_type=MESH
-        )
-
-    def greet_x(d):
-        pl.semaphore_signal(
-            barrier, 1, device_id=(re, ((x + d + 1) % 4) * 8 + z), device_id_type=MESH
-        )
-
-    for d in NEAR_RE[::-1]:
-        greet_re(d)
-    for d in NEAR[::-1]:
-        greet_z(d)
-    each(3, greet_x)
     for copy in small:
         copy.wait()
 
@@ -176,6 +176,8 @@
     g_copy.wait()
     for pp in range(2):
         phase_part(1 - core, pp)
+    for pp in range(2):
+        phase_part(core, pp)
     pl.semaphore_wait(barrier, 25)
     a1 = remote(
         acc.at[pl.ds(pl.multiple_of((1 - core) * 384, 8), 384), :], ra1,
@@ -195,10 +197,6 @@
 
     for d in NEAR:
         kz_copy(d).start()
-    for d in NEAR:
-        u1z(d).start()
-    for pp in range(2):
-        phase_part(core, pp)
 
     a1.wait_recv()
     mine = pl.multiple_of(core * 384, 8)
@@ -213,6 +211,8 @@
 
     for d in NEAR:
         a2(d).start()
+    for d in NEAR:
+        u1z(d).start()
 
     def wait_kz(d):
         src = (z + d + 1) % 8
@@ -326,9 +326,10 @@
     total = ra2[0:48, :]
     for source in range(1, 8):
         total = total + ra2[source * 48 : source * 48 + 48, :]
-    gkpad[...] = jnp.zeros_like(gkpad)
-    gkpad[pl.ds(pl.multiple_of(core * 48, 8), 48), :] = total
-    rotated = dot3(split(gkpad[...]), rotation, NN).T
+    padded = jnp.concatenate(
+        [dot3(split(total), rotation, NN), jnp.zeros((80, 128), f32)], axis=0
+    )
+    rotated = padded.T
     for ac in range(4):
         a3s[pl.ds(ac, 32, stride=4), :] = rotated[ac * 32 : ac * 32 + 32]
 
@@ -366,8 +367,6 @@
         to = ((y + d + 1) % 8) * 2 + core
         return remote(sel, q_block(re), uqs.at[d], uqr.at[y], to, pb)
 
-    for d in NEAR:
-        uq(d).start()
     usq[pl.ds(pl.multiple_of(re * 32, 8), 32), :] = sel[...]
 
     def uf(i):
@@ -384,7 +383,8 @@
     home = pl.multiple_of(pb * 48, 8)
     for n in range(2):
         v = [
-            a3r[pl.ds(n * 4 + ac, 8, stride=16), :] + a3r[pl.ds(8 + n * 4 + ac, 8, stride=16), :]
+            a3r[pl.ds(n * 4 + ac, 8, stride=16), :]
+            + pltpu.roll(a3r[pl.ds(8 + n * 4 + ac, 8, stride=16), :], 48, 1)
             for ac in range(4)
         ]
         r1, r2, r3 = pltpu.roll(v[1], 96, 1), pltpu.roll(v[2], 64, 1), pltpu.roll(v[3], 32, 1)
@@ -418,6 +418,8 @@
             bz(kh, d).start()
         for d in NEAR_X:
             bx(kh, z, d).start()
+    for d in NEAR:
+        uq(d).start()
 
     for kh in range(2):
         def pass_on(d):
@@ -546,7 +548,7 @@
     V, S, D = pltpu.VMEM, pltpu.SMEM, pltpu.SemaphoreType.DMA
     result = pl.pallas_call(
         kernel,
-        out_shape=jax.ShapeDtypeStruct((1536, 128), f32),
+        out_shape=pltpu.VMEM((1536, 128), f32),
         in_specs=[hbm] * 7,
         out_specs=vmem,
         scratch_shapes=[
@@ -569,7 +571,6 @@
             V((512, 128), f32),
             V((128, 128), f32),
             V((128, 128), f32),
-            V((128, 128), f32),
             V((1536, 128), f32),
             V((384, 128), f32),
             V((384, 384), bf16),
@@ -586,7 +587,7 @@
             D((15,)), D((16,)), D((14,)), D((16,)), D((48,)), D((64,)),
         ],
         compiler_params=pltpu.CompilerParams(
-            collective_id=0, has_side_effects=True, vmem_limit_bytes=60 * 1024 * 1024
+            collective_id=0, has_side_effects=True, vmem_limit_bytes=58 * 1024 * 1024
         ),
         name="interpolate",
     )(

time: 51.4 us -> 48.4 us (0.942)
  Pallas kernels: 49.1 us -> 47.3 us
  local copies, waits for them, and re-layouts: 2.07 us -> 0.88 us
    pallas_call x1, Pallas kernels: 49.1 us -> 47.3 us  [body(): pl.pallas_call(kernel, out_shape=pltpu.VMEM((1536, 128), f32), in_specs=[...]
    unnamed x1, local copies, waits for them, and re-layouts: 2.07 us -> 0.88 us
where the time goes in v2:
time: 48.4 us; the launch traced here: 48.2 us
  Pallas kernels  47.3 us (98%)
  local copies, waits for them, and re-layouts  0.88 us (2%)
    pallas_call x1, Pallas kernels, body(): pl.pallas_call(kernel, out_shape=pltpu.VMEM((1536, 128), f32), in_specs=[...  47.3 us

profile of v2, /device:TPU:1, one launch (start us, length us, event | category | flops | bytes accessed | tf_op | source)
XLA Modules:
  0.0 48.2 jit_solution(9683748458141525817)
XLA Ops:
  0.0 47.3 %interpolate.1 = f32[1536,128]{1,0:T(8,128)S(1)} custom-call(f32[3072,128]{1,0:T(8,128)} %bitcast.7, s32[3,32]{1,0:T(4,128)} %cells_hbm.1, s32[3,4]{1,0:T(4,128)} %pcell_hbm.1, s32[3,8]{1,0:T(4,128)} %kco_hbm.1, s32[3,128]{1,0:T(4,128)} %qco_hbm.1, f32[16,2048]{1,0:T(8,128)} %rot_hbm.1, f32[4,4608]{1,0:T(4,128)} %modes_hbm.1), custom_call_target="tpu_custom_call" | custom-call | tf_op jit(solution)/shard_map/interpolate/pallas_call | solution.py:549
  47.3 0.9 %copy.10 = f32[8,4,2,3072]{3,2,1,0:T(2,128)} copy(f32[8,4,2,3072]{3,2,1,0:T(2,128)S(1)} %bitcast.6) | data formatting | bytes 1572864

commit v3 on v2

--- a/solution.py
+++ b/solution.py
@@ -10,8 +10,8 @@
 f32, bf16, i32 = jnp.float32, jnp.bfloat16, jnp.int32
 MESH = pl.DeviceIdType.MESH
 NEAR = (0, 6, 1, 5, 2, 4, 3)
+FAR = NEAR[::-1]
 NEAR_X = (0, 2, 1)
-NEAR_RE = (0, 14, 1, 13, 2, 12, 3, 11, 4, 10, 5, 9, 6, 8, 7)
 NN = ((1,), (0,))
 NT = ((1,), (1,))
 
@@ -58,9 +58,9 @@
 def kernel(
     g_hbm, cells_hbm, pcell_hbm, kco_hbm, qco_hbm, rot_hbm, modes_hbm, out,
     cells, pcell, kco, qco, flat, modes, rot, g, acc, ra1, ra2, table, sel, kz, kx, usq, wide,
-    a3s, a3r, xs, fq, fh, fl, bh, bl, xh, xl, ys,
+    ga, turned_rows, a3s, a3r, xs, fq, fh, fl, bh, bl, xh, xl, ys,
     gsem, rotsem, insem, u1zs, u1zr, u1xs, u1xr, a1s_sem, a1r_sem, a2s_sem, a2r_sem,
-    kzs, kzr, kxs, kxr, uqs, uqr, ufs, ufr, a3s_sem, a3r_sem, bzs, bzr, bxs, bxr,
+    kzs, kzr, kxs, kxr, uqs, uqr, ufs, ufr, a4s_sem, a4r_sem, a3s_sem, a3r_sem, bzs, bzr, bxs, bxr,
 ):
     re = lax.axis_index("re")
     pb = lax.axis_index("pb")
@@ -82,8 +82,10 @@
 
     barrier = pltpu.get_barrier_semaphore()
 
-    def greet_re(d):
-        pl.semaphore_signal(barrier, 1, device_id=((re + d + 1) % 16, pb), device_id_type=MESH)
+    def greet_y(d):
+        pl.semaphore_signal(
+            barrier, 1, device_id=(((y + d + 1) % 8) * 2 + core, pb), device_id_type=MESH
+        )
 
     def greet_z(d):
         pl.semaphore_signal(
@@ -95,11 +97,11 @@
             barrier, 1, device_id=(re, ((x + d + 1) % 4) * 8 + z), device_id_type=MESH
         )
 
-    for d in NEAR_RE[::-1]:
-        greet_re(d)
     for d in NEAR[::-1]:
+        greet_y(d)
         greet_z(d)
     each(3, greet_x)
+    pl.semaphore_signal(barrier, 1, device_id=(y * 2 + (1 - core), pb), device_id_type=MESH)
     small = [
         pltpu.make_async_copy(src, dst, insem.at[i])
         for i, (src, dst) in enumerate(
@@ -178,7 +180,7 @@
         phase_part(1 - core, pp)
     for pp in range(2):
         phase_part(core, pp)
-    pl.semaphore_wait(barrier, 25)
+    pl.semaphore_wait(barrier, 18)
     a1 = remote(
         acc.at[pl.ds(pl.multiple_of((1 - core) * 384, 8), 384), :], ra1,
         a1s_sem.at[0], a1r_sem.at[0], y * 2 + (1 - core), pb,
@@ -195,7 +197,7 @@
             own_rows, own_rows, u1zs.at[d], u1zr.at[z], re, x * 8 + (z + d + 1) % 8
         )
 
-    for d in NEAR:
+    for d in FAR:
         kz_copy(d).start()
 
     a1.wait_recv()
@@ -209,7 +211,7 @@
         to = (y + d + 1) % 8
         return remote(block(ra1, to), block(ra2, y), a2s_sem.at[d], a2r_sem.at[y], to * 2 + core, pb)
 
-    for d in NEAR:
+    for d in FAR:
         a2(d).start()
     for d in NEAR:
         u1z(d).start()
@@ -326,23 +328,37 @@
     total = ra2[0:48, :]
     for source in range(1, 8):
         total = total + ra2[source * 48 : source * 48 + 48, :]
+    def half_of(which):
+        return ga.at[pl.ds(pl.multiple_of(which * 48, 8), 48), :]
+
+    half_of(core)[...] = total
+    a4 = remote(
+        half_of(core), half_of(core), a4s_sem.at[0], a4r_sem.at[0], y * 2 + (1 - core), pb
+    )
+    a4.start()
+    a4.wait_recv()
     padded = jnp.concatenate(
-        [dot3(split(total), rotation, NN), jnp.zeros((80, 128), f32)], axis=0
-    )
-    rotated = padded.T
-    for ac in range(4):
-        a3s[pl.ds(ac, 32, stride=4), :] = rotated[ac * 32 : ac * 32 + 32]
+        [dot3(split(ga[...]), rotation, NN), jnp.zeros((32, 128), f32)], axis=0
+    )
+    turned_rows[...] = padded.T
+    for n in range(2):
+        for ac in range(4):
+            a3s[pl.ds(n * 4 + ac, 8, stride=8), :] = turned_rows[
+                pl.ds(ac * 32 + 2 * core + n, 8, stride=4), :
+            ]
 
     def tile(ref, index):
         return ref.at[pl.ds(pl.multiple_of(index * 8, 8), 8), :]
 
     def a3(d):
-        to = (re + d + 1) % 16
-        return remote(tile(a3s, to), tile(a3r, re), a3s_sem.at[d], a3r_sem.at[re], to, pb)
-
-    for d in NEAR_RE:
+        to = (y + d + 1) % 8
+        return remote(
+            tile(a3s, to), tile(a3r, y), a3s_sem.at[d], a3r_sem.at[y], to * 2 + core, pb
+        )
+
+    for d in FAR:
         a3(d).start()
-    own_tile = pl.ds(pl.multiple_of(re * 8, 8), 8)
+    own_tile = pl.ds(pl.multiple_of(y * 8, 8), 8)
     a3r[own_tile, :] = a3s[own_tile, :]
 
     def wait_u1x(d):
@@ -374,17 +390,16 @@
         return remote(q_block(src), q_block(src), ufs.at[i], ufr.at[i], y * 2 + (1 - core), pb)
 
     def wait_a3(d):
-        src = (re + d + 1) % 16
-        remote(tile(a3r, src), tile(a3r, src), a3s_sem.at[0], a3r_sem.at[src], src, pb).wait_recv()
-
-    each(15, wait_a3)
+        src = (y + d + 1) % 8
+        remote(tile(a3r, src), tile(a3r, src), a3s_sem.at[0], a3r_sem.at[src], re, pb).wait_recv()
+
+    each(7, wait_a3)
 
     lane8 = iota((8, 128), 1)
     home = pl.multiple_of(pb * 48, 8)
     for n in range(2):
         v = [
-            a3r[pl.ds(n * 4 + ac, 8, stride=16), :]
-            + pltpu.roll(a3r[pl.ds(8 + n * 4 + ac, 8, stride=16), :], 48, 1)
+            a3r[pl.ds(n * 4 + ac, 8, stride=8), :]
             for ac in range(4)
         ]
         r1, r2, r3 = pltpu.roll(v[1], 96, 1), pltpu.roll(v[2], 64, 1), pltpu.roll(v[3], 32, 1)
@@ -528,7 +543,8 @@
     each(3, lambda d: kx_copy(d).wait_send())
     each(7, lambda d: uq(d).wait_send())
     each(8, lambda d: uf(d).wait_send())
-    each(15, lambda d: a3(d).wait_send())
+    a4.wait_send()
+    each(7, lambda d: a3(d).wait_send())
     for kh in range(2):
         each(7, lambda d: bz(kh, d).wait_send())
         each(24, lambda i: bx(kh, i // 3, i % 3).wait_send())
@@ -569,8 +585,10 @@
             V((64, 128), f32),
             V((512, 128), f32),
             V((512, 128), f32),
+            V((96, 128), f32),
             V((128, 128), f32),
-            V((128, 128), f32),
+            V((64, 128), f32),
+            V((64, 128), f32),
             V((1536, 128), f32),
             V((384, 128), f32),
             V((384, 384), bf16),
@@ -584,7 +602,7 @@
             D((7,)), D((8,)), D((3,)), D((4,)), D((1,)), D((1,)),
             D((7,)), D((8,)),
             D((7,)), D((8,)), D((3,)), D((4,)), D((7,)), D((8,)), D((8,)), D((8,)),
-            D((15,)), D((16,)), D((14,)), D((16,)), D((48,)), D((64,)),
+            D((1,)), D((1,)), D((7,)), D((8,)), D((14,)), D((16,)), D((48,)), D((64,)),
         ],
         compiler_params=pltpu.CompilerParams(
             collective_id=0, has_side_effects=True, vmem_limit_bytes=58 * 1024 * 1024

time: 48.4 us -> 47.5 us (0.981)
  Pallas kernels: 47.3 us -> 46.5 us
    pallas_call x1, Pallas kernels: 47.3 us -> 46.5 us  [body(): pl.pallas_call(kernel, out_shape=pltpu.VMEM((1536, 128), f32), in_specs=[...]
where the time goes in v3:
time: 47.5 us; the launch traced here: 47.4 us
  Pallas kernels  46.5 us (98%)
  local copies, waits for them, and re-layouts  0.88 us (2%)
    pallas_call x1, Pallas kernels, body(): pl.pallas_call(kernel, out_shape=pltpu.VMEM((1536, 128), f32), in_specs=[...  46.5 us

profile of v3, /device:TPU:1, one launch (start us, length us, event | category | flops | bytes accessed | tf_op | source)
XLA Modules:
  0.0 47.4 jit_solution(5309463230208744868)
XLA Ops:
  0.0 46.5 %interpolate.1 = f32[1536,128]{1,0:T(8,128)S(1)} custom-call(f32[3072,128]{1,0:T(8,128)} %bitcast.7, s32[3,32]{1,0:T(4,128)} %cells_hbm.1, s32[3,4]{1,0:T(4,128)} %pcell_hbm.1, s32[3,8]{1,0:T(4,128)} %kco_hbm.1, s32[3,128]{1,0:T(4,128)} %qco_hbm.1, f32[16,2048]{1,0:T(8,128)} %rot_hbm.1, f32[4,4608]{1,0:T(4,128)} %modes_hbm.1), custom_call_target="tpu_custom_call" | custom-call | tf_op jit(solution)/shard_map/interpolate/pallas_call | solution.py:565
  46.5 0.9 %copy.10 = f32[8,4,2,3072]{3,2,1,0:T(2,128)} copy(f32[8,4,2,3072]{3,2,1,0:T(2,128)S(1)} %bitcast.6) | data formatting | bytes 1572864

commit v4 on v3

--- a/solution.py
+++ b/solution.py
@@ -297,7 +297,7 @@
                     base = a2 * 192 + p * 24 + lo * 12
                     fq[base : base + 12, :] = cos_p * plain[i] + sin_p * crossed[i]
                     fq[base + 96 : base + 108, :] = cos_p * crossed[i] - sin_p * plain[i]
-        high, low = split(fq[...])
+        high, low = split(fq[0:384, :])
         where = pl.ds(pl.multiple_of(q * 96, 96), 96)
         fh[where, :] = dot(permute, high, NT).astype(bf16)
         fl[where, :] = dot(permute, low, NT).astype(bf16)
@@ -381,9 +381,9 @@
 
     def uq(d):
         to = ((y + d + 1) % 8) * 2 + core
-        return remote(sel, q_block(re), uqs.at[d], uqr.at[y], to, pb)
-
-    usq[pl.ds(pl.multiple_of(re * 32, 8), 32), :] = sel[...]
+        return remote(sel.at[0:32, :], q_block(re), uqs.at[d], uqr.at[y], to, pb)
+
+    usq[pl.ds(pl.multiple_of(re * 32, 8), 32), :] = sel[0:32, :]
 
     def uf(i):
         src = i * 2 + core
@@ -573,14 +573,14 @@
             S((3, 8), i32),
             S((3, 128), i32),
             V((4, 4608), f32),
-            V((144, 128), f32),
+            V((192, 128), f32),
             V((256, 128), f32),
             V((3072, 128), f32),
             V((768, 128), f32),
             V((384, 128), f32),
             V((384, 128), f32),
-            V((512, 128), f32),
-            V((32, 128), f32),
+            V((520, 128), f32),
+            V((40, 128), f32),
             V((128, 128), f32),
             V((64, 128), f32),
             V((512, 128), f32),
@@ -589,8 +589,8 @@
             V((128, 128), f32),
             V((64, 128), f32),
             V((64, 128), f32),
-            V((1536, 128), f32),
-            V((384, 128), f32),
+            V((1544, 128), f32),
+            V((392, 128), f32),
             V((384, 384), bf16),
             V((384, 384), bf16),
             V((4096, 128), bf16),

time: 47.5 us -> 47.5 us (level)
  no operation moved by 1% of the time
where the time goes in v4:
time: 47.5 us; the launch traced here: 47.4 us
  Pallas kernels  46.5 us (98%)
  local copies, waits for them, and re-layouts  0.88 us (2%)
    pallas_call x1, Pallas kernels, body(): pl.pallas_call(kernel, out_shape=pltpu.VMEM((1536, 128), f32), in_specs=[...  46.5 us

profile of v4, /device:TPU:1, one launch (start us, length us, event | category | flops | bytes accessed | tf_op | source)
XLA Modules:
  0.0 47.4 jit_solution(16641651101480424424)
XLA Ops:
  0.0 46.5 %interpolate.1 = f32[1536,128]{1,0:T(8,128)S(1)} custom-call(f32[3072,128]{1,0:T(8,128)} %bitcast.7, s32[3,32]{1,0:T(4,128)} %cells_hbm.1, s32[3,4]{1,0:T(4,128)} %pcell_hbm.1, s32[3,8]{1,0:T(4,128)} %kco_hbm.1, s32[3,128]{1,0:T(4,128)} %qco_hbm.1, f32[16,2048]{1,0:T(8,128)} %rot_hbm.1, f32[4,4608]{1,0:T(4,128)} %modes_hbm.1), custom_call_target="tpu_custom_call" | custom-call | tf_op jit(solution)/shard_map/interpolate/pallas_call | solution.py:565
  46.5 0.9 %copy.10 = f32[8,4,2,3072]{3,2,1,0:T(2,128)} copy(f32[8,4,2,3072]{3,2,1,0:T(2,128)S(1)} %bitcast.6) | data formatting | bytes 1572864

commit v5 on v4

--- a/solution.py
+++ b/solution.py
@@ -11,7 +11,7 @@
 MESH = pl.DeviceIdType.MESH
 NEAR = (0, 6, 1, 5, 2, 4, 3)
 FAR = NEAR[::-1]
-NEAR_X = (0, 2, 1)
+NEAR_X = (1, 0, 2)
 NN = ((1,), (0,))
 NT = ((1,), (1,))
 
@@ -181,24 +181,24 @@
     for pp in range(2):
         phase_part(core, pp)
     pl.semaphore_wait(barrier, 18)
+    def kz_copy(d):
+        return remote(
+            kz_block(z), kz_block(z), kzs.at[d], kzr.at[z], re, x * 8 + (z + d + 1) % 8
+        )
+
+    for d in FAR:
+        kz_copy(d).start()
     a1 = remote(
         acc.at[pl.ds(pl.multiple_of((1 - core) * 384, 8), 384), :], ra1,
         a1s_sem.at[0], a1r_sem.at[0], y * 2 + (1 - core), pb,
     )
     a1.start()
 
-    def kz_copy(d):
-        return remote(
-            kz_block(z), kz_block(z), kzs.at[d], kzr.at[z], re, x * 8 + (z + d + 1) % 8
-        )
-
     def u1z(d):
         return remote(
             own_rows, own_rows, u1zs.at[d], u1zr.at[z], re, x * 8 + (z + d + 1) % 8
         )
 
-    for d in FAR:
-        kz_copy(d).start()
 
     a1.wait_recv()
     mine = pl.multiple_of(core * 384, 8)

time: 47.5 us -> 47.5 us (level)
  no operation moved by 1% of the time
where the time goes in v5:
time: 47.5 us; the launch traced here: 47.4 us
  Pallas kernels  46.5 us (98%)
  local copies, waits for them, and re-layouts  0.88 us (2%)
    pallas_call x1, Pallas kernels, body(): pl.pallas_call(kernel, out_shape=pltpu.VMEM((1536, 128), f32), in_specs=[...  46.5 us

profile of v5, /device:TPU:1, one launch (start us, length us, event | category | flops | bytes accessed | tf_op | source)
XLA Modules:
  0.0 47.4 jit_solution(5238126628010360666)
XLA Ops:
  0.0 46.5 %interpolate.1 = f32[1536,128]{1,0:T(8,128)S(1)} custom-call(f32[3072,128]{1,0:T(8,128)} %bitcast.7, s32[3,32]{1,0:T(4,128)} %cells_hbm.1, s32[3,4]{1,0:T(4,128)} %pcell_hbm.1, s32[3,8]{1,0:T(4,128)} %kco_hbm.1, s32[3,128]{1,0:T(4,128)} %qco_hbm.1, f32[16,2048]{1,0:T(8,128)} %rot_hbm.1, f32[4,4608]{1,0:T(4,128)} %modes_hbm.1), custom_call_target="tpu_custom_call" | custom-call | tf_op jit(solution)/shard_map/interpolate/pallas_call | solution.py:565
  46.5 0.9 %copy.10 = f32[8,4,2,3072]{3,2,1,0:T(2,128)} copy(f32[8,4,2,3072]{3,2,1,0:T(2,128)S(1)} %bitcast.6) | data formatting | bytes 1572864
